TPU v7x, 32 devices: a whole 2x2x4 slice. The times are simulated.
32 devices in a mesh: gx: 8 (over y, x, core), gy: 4 (over z).
Axes of the slice: x: 2, y: 2, z: 4, core: 2. Of those that a mesh axis runs over, the one named last changes fastest.
Arguments:
- inputs: bfloat16 [32, 16, 48, 512], P(('gx', 'gy')), may hold values from -6 to 6
- grad_out: bfloat16 [32, 16, 48, 512], P(('gx', 'gy')), may hold values from -6 to 6
- conv_kernel: float32 [7, 7, 512], replicated, may hold values from -0.875 to 0.875
- conv_bias: float32 [512], replicated, may hold values from -4 to 4
- layer_norm_gain: float32 [512], replicated, may hold values from 0.1 to 1.9
- layer_norm_bias: float32 [512], replicated, may hold values from -3 to 3
- w_up: bfloat16 [512, 2048], replicated, may hold values from -0.25 to 0.25
- up_bias: float32 [2048], replicated, may hold values from -3 to 3
- w_down: bfloat16 [512, 2048], replicated, may hold values from -0.125 to 0.125
- down_bias: float32 [512], replicated, may hold values from -3 to 3
- layer_scale: float32 [512], replicated, may hold values from 0.1 to 1
Outputs:
- grad_inputs: bfloat16 [32, 16, 48, 512], P(('gx', 'gy'))
- grad_kernel: float32 [7, 7, 512], replicated
- grad_conv_bias: float32 [512], replicated
- grad_ln_gain: float32 [512], replicated
- grad_ln_bias: float32 [512], replicated
- grad_w_up: float32 [512, 2048], replicated
- grad_up_bias: float32 [2048], replicated
- grad_w_down: float32 [512, 2048], replicated
- grad_down_bias: float32 [512], replicated
- grad_layer_scale: float32 [512], replicated
All inputs are finite; a program needn't handle non-finite values.
Results may differ from a plain program's by a relative error of at most 0.0063.
Values sent between devices are 32-bit elements; how exact they have to be, the bound alone decides.
A program may use at most 128 MiB of HBM per device.

v0:
```python
import jax
import jax.numpy as jnp
from jax import lax
from jax.sharding import PartitionSpec as P


def gelu_slope(pre):
    cdf = 0.5 * (1.0 + jax.scipy.special.erf(pre * 0.7071067811865476))
    dens = jnp.exp(-0.5 * pre * pre) * 0.3989422804014327
    return cdf + pre * dens


def shards(
    inputs,
    grad_out,
    conv_kernel,
    conv_bias,
    layer_norm_gain,
    layer_norm_bias,
    w_up,
    up_bias,
    w_down,
    down_bias,
    layer_scale,
):
    image = inputs[0].astype(jnp.float32)
    row_count, column_count, channel_count = image.shape
    ksize = conv_kernel.shape[0]
    padded = jnp.pad(image, ((3, 3), (3, 3), (0, 0)))
    mixed = jnp.zeros_like(image) + conv_bias
    for i in range(ksize):
        for j in range(ksize):
            mixed = mixed + padded[i : i + row_count, j : j + column_count] * conv_kernel[i, j]
    mean_removed = mixed - jnp.mean(mixed, axis=-1, keepdims=True)
    inverse_deviation = lax.rsqrt(
        jnp.mean(mean_removed * mean_removed, axis=-1, keepdims=True) + 1e-06
    )
    standardized_input = mean_removed * inverse_deviation
    normalized_output = (
        (standardized_input * layer_norm_gain + layer_norm_bias)
        .astype(jnp.bfloat16)
        .reshape(row_count * column_count, channel_count)
    )
    pre = jnp.dot(normalized_output, w_up, preferred_element_type=jnp.float32) + up_bias
    hidden = jax.nn.gelu(pre, approximate=False).astype(jnp.bfloat16)
    branch = (
        lax.dot_general(
            hidden, w_down, (((1,), (1,)), ((), ())), preferred_element_type=jnp.float32
        )
        + down_bias
    )
    upstream = grad_out[0].astype(jnp.float32).reshape(row_count * column_count, channel_count)
    devices = lax.axis_size("gx") * lax.axis_size("gy")
    image_fraction = 1.0 / devices
    g_scale = jnp.sum(upstream * branch, axis=0) * image_fraction
    g_branch = (upstream * layer_scale).astype(jnp.bfloat16)
    gw_down = (
        lax.dot_general(
            g_branch, hidden, (((0,), (0,)), ((), ())), preferred_element_type=jnp.float32
        )
        * image_fraction
    )
    g_down_bias = jnp.sum(g_branch.astype(jnp.float32), axis=0) * image_fraction
    g_hidden = jnp.dot(g_branch, w_down, preferred_element_type=jnp.float32)
    g_pre = (g_hidden * gelu_slope(pre)).astype(jnp.bfloat16)
    gw_up = (
        lax.dot_general(
            normalized_output, g_pre, (((0,), (0,)), ((), ())), preferred_element_type=jnp.float32
        )
        * image_fraction
    )
    half = (
        lax.psum_scatter(gw_up, "gx", scatter_dimension=0, tiled=True),
        lax.psum_scatter(gw_down, "gx", scatter_dimension=0, tiled=True),
    )
    parts = (
        lax.psum_scatter(half[0], "gy", scatter_dimension=1, tiled=True),
        lax.psum_scatter(half[1], "gy", scatter_dimension=1, tiled=True),
    )
    g_up_bias = jnp.sum(g_pre.astype(jnp.float32), axis=0) * image_fraction
    normalized_gradient = lax.dot_general(
        g_pre, w_up, (((1,), (1,)), ((), ())), preferred_element_type=jnp.float32
    ).reshape(row_count, column_count, channel_count)
    gain_gradient = jnp.sum(normalized_gradient * standardized_input, axis=(0, 1)) * image_fraction
    g_lnbias = jnp.sum(normalized_gradient, axis=(0, 1)) * image_fraction
    gradient_times_normalized = normalized_gradient * layer_norm_gain
    mixed_gradient = inverse_deviation * (
        gradient_times_normalized
        - jnp.mean(gradient_times_normalized, axis=-1, keepdims=True)
        - standardized_input
        * jnp.mean(gradient_times_normalized * standardized_input, axis=-1, keepdims=True)
    )
    g_cbias = jnp.sum(mixed_gradient, axis=(0, 1)) * image_fraction
    kernel_terms = []
    for i in range(ksize):
        for j in range(ksize):
            kernel_terms.append(
                jnp.sum(
                    mixed_gradient * padded[i : i + row_count, j : j + column_count], axis=(0, 1)
                )
            )
    g_kernel = jnp.stack(kernel_terms).reshape(ksize, ksize, channel_count) * image_fraction
    gpad = jnp.pad(mixed_gradient, ((3, 3), (3, 3), (0, 0)))
    back = grad_out[0].astype(jnp.float32)
    for i in range(ksize):
        for j in range(ksize):
            back = (
                back
                + gpad[6 - i : 6 - i + row_count, 6 - j : 6 - j + column_count] * conv_kernel[i, j]
            )
    grad_inputs = back.astype(jnp.bfloat16).reshape(1, row_count, column_count, channel_count)
    small = lax.psum(
        (g_kernel, g_cbias, gain_gradient, g_lnbias, g_up_bias, g_down_bias, g_scale), ("gx", "gy")
    )
    half_back = (
        lax.all_gather(parts[0], "gy", axis=1, tiled=True),
        lax.all_gather(parts[1], "gy", axis=1, tiled=True),
    )
    whole = (
        lax.all_gather(half_back[0], "gx", axis=0, tiled=True),
        lax.all_gather(half_back[1], "gx", axis=0, tiled=True),
    )
    return (
        grad_inputs,
        small[0],
        small[1],
        small[2],
        small[3],
        whole[0],
        small[4],
        whole[1],
        small[5],
        small[6],
    )


def solution(mesh):
    placed = (
        P(("gx", "gy"), None, None, None),
        P(("gx", "gy"), None, None, None),
        P(),
        P(),
        P(),
        P(),
        P(),
        P(),
        P(),
        P(),
        P(),
    )
    return jax.shard_map(
        shards,
        mesh=mesh,
        in_specs=placed,
        out_specs=(P(("gx", "gy"), None, None, None), P(), P(), P(), P(), P(), P(), P(), P(), P()),
        check_vma=False,
    )
```

profile of v0, /device:TPU:1, one launch (start us, length us, event | category | flops | bytes accessed | tf_op | source)
XLA Modules:
  0.0 388.0 jit_solution(16920559950376199398)
XLA Ops:
  8.1 1.0 fusion.123
  9.1 1.2 fusion.121
  10.3 1.2 fusion.122
  11.5 1.3 bitcast_convert_fusion
  12.8 11.8 %fusion.120 = (f32[16,48]{1,0:T(8,128)S(1)}, f32[16,48,512]{2,1,0:T(8,128)S(1)}) fusion(f32[512]{0:T(512)S(1)} %bitcast.158, f32[512]{0:T(512)S(1)} %bitcast.160, f32[512]{0:T(512)S(1)} %bitcast.164, f32[512]{0:T(512)S(1)} %bitcast.166, f32[512]{0:T(512)S(1)} %bitcast.168, f32[512]{0:T(512)S(1)} %bitcast.170, f32[512]{0:T(512)S(1)} %bitcast.172, ...), kind=kLoop, calls=%fused_computation.303 | loop fusion | flops 38927616 | bytes 3251200 | tf_op jit(solution)/shard_map/reduce_sum | solution.py:34
  24.7 0.3 multiply_reduce_fusion.52
  25.1 1.3 copy-done.8
  26.9 0.4 copy-done.17
  27.3 16.1 %fusion.8 = (bf16[768,2048]{1,0:T(8,128)(2,1)}, f32[768,2048]{1,0:T(8,128)S(1)}) fusion(f32[2048]{0:T(1024)S(1)} %copy-done.17, bf16[768,512]{1,0:T(8,128)(2,1)S(1)} %bitcast.138, bf16[512,2048]{1,0:T(8,128)(2,1)S(1)} %copy-done), kind=kOutput, calls=%fused_computation.106 | convolution fusion | flops 1714421760 | bytes 12328960 | tf_op jit(solution)/shard_map/dot_general | solution.py:44
  43.4 4.2 %convert_reduce_fusion = (f32[2048]{0:T(1024)S(1)}, bf16[768,2048]{1,0:T(8,128)(2,1)S(1)}) fusion(f32[768,2048]{1,0:T(8,128)S(1)} %get-tuple-element.138, f32[2048]{0:T(1024)S(1)} %copy-done.17, bf16[768,512]{1,0:T(8,128)(2,1)S(1)} %fusion.115, bf16[512,2048]{1,0:T(8,128)(2,1)S(1)} %copy-done.16), kind=kOutput, calls=%fused_computation.120 | convolution fusion | flops 1631057920 | bytes 12337152 | tf_op jit(solution)/shard_map/dot_general | solution.py:64
  47.6 1.7 copy-done.7
  49.4 3.8 convolution_multiply_fusion.1
  53.3 6.0 %convolution_multiply_fusion = f32[512,2048]{1,0:T(8,128)} fusion(bf16[768,512]{1,0:T(8,128)(2,1)} %copy-done.9, bf16[768,2048]{1,0:T(8,128)(2,1)} %get-tuple-element.137), kind=kOutput, calls=%fused_computation.123 | convolution fusion | flops 1611661312 | bytes 8126464 | tf_op jit(solution)/shard_map/dot_general | solution.py:58
  59.3 47.4 %reduce-scatter.5.cloned.1.call-done = f32[64,2048]{1,0:T(8,128)} async-done(((f32[512,2048]{1,0:T(8,128)}), f32[64,2048]{1,0:T(8,128)}) %reduce-scatter.5.cloned.1.call-update) | async-done | bytes 524304 | tf_op jit(solution)/shard_map/reduce_scatter | solution.py:73
  106.9 55.6 %reduce-scatter.9.cloned.1.call-done = f32[64,2048]{1,0:T(8,128)} async-done(((f32[512,2048]{1,0:T(8,128)}), f32[64,2048]{1,0:T(8,128)}) %reduce-scatter.9.cloned.1.call-update) | async-done | bytes 524304 | tf_op jit(solution)/shard_map/reduce_scatter | solution.py:74
  162.5 22.0 %reduce-scatter.7.cloned.1.call-done = f32[64,512]{1,0:T(8,128)} async-done(((f32[64,2048]{1,0:T(8,128)}), f32[64,512]{1,0:T(8,128)}) %reduce-scatter.7.cloned.1.call-update) | async-done | bytes 131088 | tf_op jit(solution)/shard_map/reduce_scatter | solution.py:77
  184.5 17.2 %all_gather.12 = f32[64,2048]{1,0:T(8,128)} all-gather(f32[64,512]{1,0:T(8,128)} %reduce-scatter.7.cloned.1.call-done), channel_id=1, replica_groups=mesh['gx'=8,'gy'=4] {'gy'}, dimensions={1}, use_global_device_ids=true | all-gather | bytes 655360 | tf_op jit(solution)/shard_map/all_gather | solution.py:116
  201.7 7.9 %reduce-scatter.11.cloned.1.call-done = f32[64,512]{1,0:T(8,128)} async-done(((f32[64,2048]{1,0:T(8,128)}), f32[64,512]{1,0:T(8,128)}) %reduce-scatter.11.cloned.1.call-update) | async-done | bytes 131088 | tf_op jit(solution)/shard_map/reduce_scatter | solution.py:78
  209.6 14.2 %all_gather.14 = f32[64,2048]{1,0:T(8,128)} all-gather(f32[64,512]{1,0:T(8,128)} %reduce-scatter.11.cloned.1.call-done), channel_id=1, replica_groups=mesh['gx'=8,'gy'=4] {'gy'}, dimensions={1}, use_global_device_ids=true | all-gather | bytes 655360 | tf_op jit(solution)/shard_map/all_gather | solution.py:117
  224.0 4.9 %fusion.118 = (f32[512]{0:T(512)S(1)}, f32[768]{0:T(1024)S(1)}, f32[768,512]{1,0:T(8,128)}) fusion(f32[512]{0:T(512)S(1)} %copy-done.12, bf16[768,2048]{1,0:T(8,128)(2,1)} %copy-done.7, bf16[512,2048]{1,0:T(8,128)(2,1)S(1)} %copy-done), kind=kOutput, calls=%fused_computation.301 | convolution fusion | flops 1611791104 | bytes 6822912 | tf_op jit(solution)/shard_map/dot_general | solution.py:81
  229.0 2.6 multiply_reduce_fusion
  231.8 6.8 %multiply_reduce_fusion.1 = (f32[512]{0:T(512)S(1)}, f32[512]{0:T(512)S(1)}, f32[512]{0:T(512)S(1)}, f32[512]{0:T(512)S(1)}, f32[512]{0:T(512)S(1)}, /*index=5*/...) fusion(f32[16,48,512]{2,1,0:T(8,128)S(1)} %copy-done.4, ...), kind=kLoop, calls=%fused_computation.232 | loop fusion | flops 16899072 | bytes 6342656 | tf_op jit(solution)/shard_map/reduce_sum | solution.py:98
  238.7 2.4 fusion.119
  241.1 3.6 multiply_reduce_fusion.19
  244.9 0.7 mul.1339
  245.6 37.9 %fusion.117 = bf16[1,16,48,512]{3,2,1,0:T(8,128)(2,1)} fusion(f32[512]{0:T(512)S(1)} %bitcast.159, f32[16,48,512]{2,1,0:T(8,128)} %copy-done.5, f32[512]{0:T(512)S(1)} %bitcast.161, f32[512]{0:T(512)S(1)} %bitcast.165, f32[512]{0:T(512)S(1)} %bitcast.167, f32[512]{0:T(512)S(1)} %bitcast.169, f32[512]{0:T(512)S(1)} %bitcast.171, f32[512]{0:T(512)S(1)} %bitcast.173, ...), kind=kLoop, calls=%fused_computation.289 | loop fusion | flops 39321600 | bytes 3246080 | tf_op jit(solution)/shard_map/reshape | solution.py:111
  283.8 3.4 fusion.116
  287.2 42.0 %all-reduce.2 = (f32[512]{0:T(512)}, f32[512]{0:T(512)}, f32[512]{0:T(512)}, f32[2048]{0:T(1024)}, f32[512]{0:T(512)}, /*index=5*/f32[512]{0:T(512)}) all-reduce(f32[512]{0:T(512)S(1)} %broadcast_multiply_fusion.9, f32[512]{0:T(512)S(1)} %get-tuple-element.142, ...), channel_id=1, replica_groups=mesh['gx'=8,'gy'=4] {'gx','gy'}, use_global_device_ids=true, to_apply=%region_55.56 | all-reduce | flops 4608 | bytes 36864 | tf_op jit(solution)/shard_map/psum | solution.py:112
  329.3 42.8 %all-reduce.5.cloned.1.call-done = f32[7,7,512]{2,1,0:T(8,128)} async-done(((f32[7,7,512]{2,1,0:T(8,128)}), f32[7,7,512]{2,1,0:T(8,128)}) %all-reduce.5.cloned.1.call-update) | async-done | bytes 100368 | tf_op jit(solution)/shard_map/psum | solution.py:112
  372.1 1.6 copy.24
  373.7 4.8 %copy.25 = f32[512,2048]{1,0:T(8,128)} copy(f32[512,2048]{1,0:T(8,128)} %all-gather.3.cloned.1.call-done) | data formatting | bytes 8388608
  378.5 2.0 copy.26
  (65 shorter events, 1.9 us)
Async XLA Ops:
  8.0 18.9 %copy-start = (bf16[512,2048]{1,0:T(8,128)(2,1)S(1)}, bf16[512,2048]{1,0:T(8,128)(2,1)}, u32[]{:S(2)}) copy-start(bf16[512,2048]{1,0:T(8,128)(2,1)} %param.17) | copy-start | bytes 6291460
  8.0 4.8 %copy-start.14 = (f32[512]{0:T(512)S(1)}, f32[512]{0:T(512)}, u32[]{:S(2)}) copy-start(f32[512]{0:T(512)} %param.14) | copy-start | bytes 6148
  8.0 98.8 %reduce-scatter.5.cloned.1.call-start = ((), (), s32[]{:S(2)}) async-start(), calls=%async_computation.5 | async-start | bytes 4718592 | tf_op jit(solution)/shard_map/reduce_scatter | solution.py:73
  12.8 11.8 %copy-start.3 = (f32[16,48,512]{2,1,0:T(8,128)}, f32[16,48,512]{2,1,0:T(8,128)S(1)}, u32[]{:S(2)}) copy-start(f32[16,48,512]{2,1,0:T(8,128)S(1)} %bitcast_convert_fusion) | copy-start | bytes 4718596
  24.6 1.9 copy-start.1
  24.7 1.7 copy-start.8
  24.7 1.7 copy-start.13
  24.7 1.8 copy-start.12
  24.7 1.8 copy-start.15
  26.5 16.8 %copy-start.9 = (bf16[768,512]{1,0:T(8,128)(2,1)}, bf16[768,512]{1,0:T(8,128)(2,1)S(1)}, u32[]{:S(2)}) copy-start(bf16[768,512]{1,0:T(8,128)(2,1)S(1)} %fusion.115) | copy-start | bytes 2359300
  26.6 0.7 copy-start.17
  27.3 16.1 %copy-start.16 = (bf16[512,2048]{1,0:T(8,128)(2,1)S(1)}, bf16[512,2048]{1,0:T(8,128)(2,1)}, u32[]{:S(2)}) copy-start(bf16[512,2048]{1,0:T(8,128)(2,1)} %param.19) | copy-start | bytes 6291460
  47.6 1.7 copy-start.7
  53.2 109.2 %reduce-scatter.9.cloned.1.call-start = ((), (), s32[]{:S(2)}) async-start(), calls=%async_computation.8 | async-start | bytes 4718592 | tf_op jit(solution)/shard_map/reduce_scatter | solution.py:74
  59.3 125.2 %reduce-scatter.7.cloned.1.call-start = ((), (), s32[]{:S(2)}) async-start(), calls=%async_computation.6 | async-start | bytes 655360 | tf_op jit(solution)/shard_map/reduce_scatter | solution.py:77
  106.8 102.8 %reduce-scatter.11.cloned.1.call-start = ((), (), s32[]{:S(2)}) async-start(), calls=%async_computation.9 | async-start | bytes 655360 | tf_op jit(solution)/shard_map/reduce_scatter | solution.py:78
  162.5 166.8 %all-gather.3.cloned.1.call-start = ((), (), s32[]{:S(2)}) async-start(), calls=%async_computation.7 | async-start | bytes 4718592 | tf_op jit(solution)/shard_map/all_gather | solution.py:120
  201.7 127.6 %all-gather.5.cloned.1.call-start = ((), (), s32[]{:S(2)}) async-start(), calls=%async_computation.10 | async-start | bytes 4718592 | tf_op jit(solution)/shard_map/all_gather | solution.py:121
  223.8 148.3 %all-reduce.5.cloned.1.call-start = ((), (), s32[]{:S(2)}) async-start(), calls=%async_computation.4 | async-start | bytes 229376 | tf_op jit(solution)/shard_map/psum | solution.py:112
  229.0 2.6 copy-start.2
  229.0 2.8 copy-start.4
  231.8 6.9 %copy-start.11 = (bf16[1,16,48,512]{3,2,1,0:T(8,128)(2,1)S(1)}, bf16[1,16,48,512]{3,2,1,0:T(8,128)(2,1)}, u32[]{:S(2)}) copy-start(bf16[1,16,48,512]{3,2,1,0:T(8,128)(2,1)} %param.11) | copy-start | bytes 2359300
  238.7 2.4 copy-start.5
  245.6 38.2 %copy-start.6 = (bf16[768,2048]{1,0:T(8,128)(2,1)S(1)}, bf16[768,2048]{1,0:T(8,128)(2,1)}, u32[]{:S(2)}) copy-start(bf16[768,2048]{1,0:T(8,128)(2,1)} %get-tuple-element.137) | copy-start | bytes 9437188
  245.6 38.2 %copy-start.18 = (f32[512]{0:T(512)S(1)}, f32[512]{0:T(512)}, u32[]{:S(2)}) copy-start(f32[512]{0:T(512)} %param.20) | copy-start | bytes 6148
  373.6 4.9 %copy-start.10 = (f32[512,2048]{1,0:T(8,128)S(1)}, f32[512,2048]{1,0:T(8,128)}, u32[]{:S(2)}) copy-start(f32[512,2048]{1,0:T(8,128)} %all-gather.5.cloned.1.call-done) | copy-start | bytes 12582916
Sparse Core Ops, SparseCore 0:
  53.4 53.3 reduce-scatter.4
  111.1 51.3 reduce-scatter.8
  164.7 19.7 reduce-scatter.6
  186.6 22.9 reduce-scatter.10
  211.3 37.5 all-gather.2
  250.7 36.8 all-gather.4
Sparse Core Ops, SparseCore 1:
  245.7 126.4 all-reduce.4
where the time goes:
time: 389 us; the launch traced here: 388 us
  waiting for transfers between devices  176 us (45%)
  blocking collectives  73.4 us (19%)
  other arithmetic  67.5 us (17%)
  matrix products  38.5 us (10%)
  local copies, waits for them, and re-layouts  16.5 us (4%)
  between operations  15.9 us (4%)
    reduce_scatter x1, waiting for transfers between devices, shards(): lax.psum_scatter(gw_down, 'gx', scatter_dimension=0, tiled=True)  55.6 us
    reduce_scatter x1, waiting for transfers between devices, shards(): lax.psum_scatter(gw_up, 'gx', scatter_dimension=0, tiled=True)  47.4 us
    psum x1, waiting for transfers between devices, shards(): lax.psum((g_kernel, g_cbias, gain_gradient, g_lnbias, g_up_bias, g_down_b...  42.8 us
    psum x1, blocking collectives, shards(): lax.psum((g_kernel, g_cbias, gain_gradient, g_lnbias, g_up_bias, g_down_b...  42 us
    reshape x1, other arithmetic, shards(): back.astype(jnp.bfloat16).reshape(1, row_count, column_count, channel_count)  37.9 us
    reduce_scatter x1, waiting for transfers between devices, shards(): lax.psum_scatter(half[0], 'gy', scatter_dimension=1, tiled=True)  22 us
    all_gather x1, blocking collectives, shards(): lax.all_gather(parts[0], 'gy', axis=1, tiled=True)  17.2 us
    dot_general x1, matrix products, shards(): jnp.dot(normalized_output, w_up, preferred_element_type=jnp.float32)  16.1 us
  transfers between devices with their start and end apart: 7, of which 5 were waited for; matrix products, arithmetic and copies ran while one was open for 18% of the time, Pallas kernels for 0%

commit v1 on v0

v1 whole, which is shorter than its diff:
```python
import functools

import jax
import jax.numpy as jnp
from jax import lax
from jax.experimental import pallas as pl
from jax.experimental.pallas import tpu as pltpu
from jax.sharding import PartitionSpec as P

MESH = pl.DeviceIdType.MESH
LANES = 128
MARGIN = 8
F32 = jnp.float32
BF16 = jnp.bfloat16


def fill_padded(pad, rows, columns, half, read):
    pad[...] = jnp.zeros_like(pad)

    def put(h, _):
        pad[h + half, MARGIN : MARGIN + columns, :] = read(h)
        return 0

    lax.fori_loop(0, rows, put, 0)


def fill_shifts(shifts, pad, lanes, ksize, columns):
    half = ksize // 2

    def put(r, _):
        for j in range(ksize):
            start = MARGIN - half + j
            shifts[j, r] = pad[r, start : start + columns, lanes]
        return 0

    lax.fori_loop(0, pad.shape[0], put, 0)


def block_kernel(
    rows,
    columns,
    ksize,
    x_ref,
    up_ref,
    k_ref,
    cbias_ref,
    gain_ref,
    lnb_ref,
    wup_ref,
    upb_ref,
    wdown_ref,
    downb_ref,
    scale_ref,
    gmixed_ref,
    gwup_ref,
    gwdown_ref,
    small_ref,
    pad,
    shifts,
    xhat,
    inv,
    normed,
    normed_t,
    gb,
    gb_t,
    hid,
    gpre,
    gnormed,
):
    pixels, channels = xhat.shape
    hidden_units = wup_ref.shape[1]
    half = ksize // 2
    fill_padded(pad, rows, columns, half, lambda h: x_ref[h].astype(F32))
    for cb in range(channels // LANES):
        lanes = slice(cb * LANES, (cb + 1) * LANES)
        fill_shifts(shifts, pad, lanes, ksize, columns)

        def conv_row(h, _):
            total = jnp.zeros((columns, LANES), F32) + cbias_ref[:, lanes]
            for i in range(ksize):
                for j in range(ksize):
                    tap = i * ksize + j
                    total = total + shifts[j, h + i] * k_ref[tap : tap + 1, lanes]
            xhat[pl.ds(pl.multiple_of(h * columns, 8), columns), lanes] = total
            return 0

        lax.fori_loop(0, rows, conv_row, 0)

    step = columns * 2
    gain = gain_ref[...]
    small_ref[...] = jnp.zeros_like(small_ref)

    def norm_rows(b, carry):
        sum_up, sum_gb = carry
        at = pl.ds(pl.multiple_of(b * step, 16), step)
        mixed = xhat[at, :]
        removed = mixed - jnp.mean(mixed, axis=-1, keepdims=True)
        deviation = lax.rsqrt(jnp.mean(removed * removed, axis=-1, keepdims=True) + 1e-06)
        standard = removed * deviation
        xhat[at, :] = standard
        inv[at, :] = deviation
        normed[at, :] = (standard * gain + lnb_ref[...]).astype(BF16)
        upstream = up_ref[at, :].astype(F32)
        g_branch = (upstream * scale_ref[...]).astype(BF16)
        gb[at, :] = g_branch
        sum_up = sum_up + jnp.sum(upstream, axis=0, keepdims=True)
        sum_gb = sum_gb + jnp.sum(g_branch.astype(F32), axis=0, keepdims=True)
        return sum_up, sum_gb

    zero = jnp.zeros((1, channels), F32)
    sum_up, sum_gb = lax.fori_loop(0, pixels // step, norm_rows, (zero, zero))
    normed_t[...] = jnp.transpose(normed[...].astype(F32)).astype(BF16)
    gb_t[...] = jnp.transpose(gb[...].astype(F32)).astype(BF16)
    gnormed[...] = jnp.zeros_like(gnormed)
    block = channels
    small_ref[4:5, :] = sum_gb
    tall = pixels // 3

    folded = jnp.zeros((channels, LANES), F32)
    for fb in range(hidden_units // block):
        cols = slice(fb * block, (fb + 1) * block)
        bias = upb_ref[:, cols]

        def mlp_rows(b, total):
            at = pl.ds(pl.multiple_of(b * tall, 16), tall)
            pre = jnp.dot(normed[at, :], wup_ref[:, cols], preferred_element_type=F32) + bias
            cdf = 0.5 * (1.0 + lax.erf(pre * 0.7071067811865476))
            hid[at, :] = (pre * cdf).astype(BF16)
            slope = cdf + pre * (jnp.exp(-0.5 * pre * pre) * 0.3989422804014327)
            g_hidden = jnp.dot(gb[at, :], wdown_ref[:, cols], preferred_element_type=F32)
            g = (g_hidden * slope).astype(BF16)
            gpre[at, :] = g
            gnormed[at, :] += lax.dot_general(
                g, wup_ref[:, cols], (((1,), (1,)), ((), ())), preferred_element_type=F32
            )
            return total + jnp.sum(g.astype(F32), axis=0, keepdims=True)

        total = lax.fori_loop(0, 3, mlp_rows, jnp.zeros((1, block), F32))
        small_ref[6 + fb : 7 + fb, :] = total
        gwup_ref[:, cols] = jnp.dot(normed_t[...], gpre[...], preferred_element_type=F32)
        gw = jnp.dot(gb_t[...], hid[...], preferred_element_type=F32)
        gwdown_ref[:, cols] = gw
        product = gw * wdown_ref[:, cols].astype(F32)
        for part in range(block // LANES):
            folded = folded + product[:, part * LANES : (part + 1) * LANES]

    scale_sum = jnp.sum(jnp.transpose(folded), axis=0, keepdims=True)
    small_ref[5:6, :] = scale_sum / scale_ref[...] + downb_ref[...] * sum_up

    def back_rows(b, carry):
        s_gain, s_bias, s_conv = carry
        at = pl.ds(pl.multiple_of(b * step, 16), step)
        g, standard = gnormed[at, :], xhat[at, :]
        gx = g * gain
        mean_g = jnp.mean(gx, axis=-1, keepdims=True)
        mean_gx = jnp.mean(gx * standard, axis=-1, keepdims=True)
        gm = inv[at, :] * (gx - mean_g - standard * mean_gx)
        gmixed_ref[at, :] = gm
        return (
            s_gain + jnp.sum(g * standard, axis=0, keepdims=True),
            s_bias + jnp.sum(g, axis=0, keepdims=True),
            s_conv + jnp.sum(gm, axis=0, keepdims=True),
        )

    s_gain, s_bias, s_conv = lax.fori_loop(0, pixels // step, back_rows, (zero, zero, zero))
    small_ref[1:2, :] = s_conv
    small_ref[2:3, :] = s_gain
    small_ref[3:4, :] = s_bias


def add_rows(target, at, source, source_at, count, cols):
    def one(r, _):
        to = pl.ds(pl.multiple_of(at + r * 8, 8), 8)
        here = pl.ds(pl.multiple_of(source_at + r * 8, 8), 8)
        target[to, :] += source[here, cols]
        return 0

    lax.fori_loop(0, count // 8, one, 0)


def piece_shape(size, width, parts):
    across = min(parts, width // LANES)
    return across, size * across // parts, width // across


def reduce_steps(gx_count, gy_count, order, acc, out, base, width, recv, zrecv, sends, recvs, pending):
    gi, zi = lax.axis_index("gx"), lax.axis_index("gy")
    fraction = 1.0 / (gx_count * gy_count)
    all_cols = slice(base, base + width)
    slot = [0]

    def send(src, dst, gx_to, gy_to):
        n = slot[0]
        slot[0] += 1
        copy = pltpu.make_async_remote_copy(
            src_ref=src,
            dst_ref=dst,
            send_sem=sends.at[n],
            recv_sem=recvs.at[n],
            device_id=(gx_to, gy_to),
            device_id_type=MESH,
        )
        copy.start()
        pending.append(copy)
        return copy

    def rows_at(at, n):
        return pl.ds(pl.multiple_of(at, 8), n)

    size, at, filled = acc.shape[0], 0, 0
    source, source_at, cols = acc, 0, all_cols
    for b in order:
        bit = (gi // 2**b) % 2
        other = gi + (1 - 2 * bit) * 2**b
        size //= 2
        give = source.at[rows_at(source_at + (1 - bit) * size, size), cols]
        copy = send(give, recv.at[filled : filled + size, :], other, zi)
        yield
        copy.wait_recv()
        add_rows(recv, filled, source, source_at + bit * size, size, cols)
        source, source_at, cols = recv, filled, slice(0, width)
        filled += size
        at = at + bit * size

    across, prows, pcols = piece_shape(size, width, gy_count)

    def piece(ref, z, top, left):
        there = rows_at(top + (z // across) * prows, prows)
        return ref.at[there, pl.ds(pl.multiple_of(left + (z % across) * pcols, LANES), pcols)]

    copies = []
    for d in range(1, gy_count):
        z = (zi + d) % gy_count
        copies.append(send(piece(recv, z, source_at, 0), zrecv.at[d - 1], gi, z))
    yield
    total = piece(recv, zi, source_at, 0)[...]
    for d in range(1, gy_count):
        copies[d - 1].wait_recv()
        total = total + zrecv[d - 1]
    done = piece(out, zi, at, base)
    done[...] = total * fraction
    copies = []
    for d in range(1, gy_count):
        z = (zi + d) % gy_count
        copies.append(send(done, done, gi, z))
    yield
    for copy in copies:
        copy.wait_recv()
    for b in reversed(order):
        bit = (gi // 2**b) % 2
        other = gi + (1 - 2 * bit) * 2**b
        mine = out.at[rows_at(at, size), all_cols]
        copy = send(mine, mine, other, zi)
        at = at - bit * size
        size *= 2
        yield
        copy.wait_recv()


def reduce_kernel(
    gx_count,
    gy_count,
    chunks,
    rows,
    columns,
    ksize,
    gwup_ref,
    gwdown_ref,
    small_ref,
    gm_ref,
    x_ref,
    up_ref,
    k_ref,
    back_ref,
    out_up,
    out_down,
    out_small,
    pad_x,
    pad_g,
    shift_x,
    shift_g,
    acc_small,
    recv,
    zrecv,
    recv_small,
    zrecv_small,
    sends,
    recvs,
):
    gi, zi = lax.axis_index("gx"), lax.axis_index("gy")
    half = ksize // 2
    channels = k_ref.shape[1]
    bits = (gx_count - 1).bit_length()
    barrier = pltpu.get_barrier_semaphore()
    for b in range(bits):
        bit = (gi // 2**b) % 2
        other = gi + (1 - 2 * bit) * 2**b
        pl.semaphore_signal(barrier, inc=1, device_id=(other, zi), device_id_type=MESH)
    for d in range(1, gy_count):
        z = (zi + d) % gy_count
        pl.semaphore_signal(barrier, inc=1, device_id=(gi, z), device_id_type=MESH)
    pl.semaphore_wait(barrier, bits + gy_count - 1)

    pending = []
    orders = ([0] + list(range(1, bits)), [0] + list(range(bits - 1, 0, -1)))
    width = gwup_ref.shape[1] * 2 // chunks
    steps = []
    for n in range(chunks):
        acc, out = (gwdown_ref, out_down) if n % 2 == 0 else (gwup_ref, out_up)
        steps.append(
            reduce_steps(
                gx_count, gy_count, orders[n % 2], acc, out, (n // 2) * width, width,
                recv.at[n], zrecv.at[n], sends.at[n], recvs.at[n], pending,
            )
        )
    steps.append(
        reduce_steps(
            gx_count, gy_count, orders[0], acc_small, out_small, 0, LANES,
            recv_small, zrecv_small, sends.at[chunks], recvs.at[chunks], pending,
        )
    )

    def prepare():
        fill_padded(pad_x, rows, columns, half, lambda h: x_ref[h].astype(F32))
        fill_padded(pad_g, rows, columns, half, lambda h: gm_ref[h])
        acc_small[...] = jnp.zeros_like(acc_small)

    def conv_block(cb):
        lanes = slice(cb * LANES, (cb + 1) * LANES)
        fill_shifts(shift_x, pad_x, lanes, ksize, columns)
        fill_shifts(shift_g, pad_g, lanes, ksize, columns)
        base = cb * 64
        acc_small[base + 48 : base + 64, :] = small_ref[:, lanes]

        def back_row(h, _):
            total = up_ref[h, :, lanes].astype(F32)
            for i in range(ksize):
                for j in range(ksize):
                    tap = i * ksize + j
                    total = total + (
                        shift_g[ksize - 1 - j, h + (ksize - 1 - i)] * k_ref[tap : tap + 1, lanes]
                    )
            back_ref[h, :, lanes] = total.astype(BF16)
            return 0

        lax.fori_loop(0, rows, back_row, 0)
        for j in range(ksize):

            def kernel_row(h, sums):
                g = shift_g[half, h + half]
                new = []
                for i in range(ksize):
                    p = g * shift_x[j, h + i]
                    part = p[0:8]
                    for w in range(8, columns, 8):
                        part = part + p[w : w + 8]
                    new.append(sums[i] + part)
                return tuple(new)

            zeros = tuple(jnp.zeros((8, LANES), F32) for _ in range(ksize))
            sums = lax.fori_loop(0, rows, kernel_row, zeros)
            for i in range(ksize):
                row = base + i * ksize + j
                acc_small[row : row + 1, :] = jnp.sum(sums[i], axis=0, keepdims=True)

    blocks = channels // LANES
    work = {0: [prepare]}
    for cb in range(blocks):
        work.setdefault(cb, []).append(functools.partial(conv_block, cb))
    begin = [(n // 2) * 2 for n in range(chunks)] + [blocks]
    live = list(enumerate(steps))
    tick = 0
    while live:
        left = []
        for n, step in live:
            if tick < begin[n]:
                left.append((n, step))
                continue
            try:
                next(step)
                left.append((n, step))
            except StopIteration:
                pass
        live = left
        for job in work.get(tick, []):
            job()
        tick += 1
    for copy in pending:
        copy.wait_send()


def shards(
    gx_count,
    gy_count,
    inputs,
    grad_out,
    conv_kernel,
    conv_bias,
    layer_norm_gain,
    layer_norm_bias,
    w_up,
    up_bias,
    w_down,
    down_bias,
    layer_scale,
):
    _, rows, columns, channels = inputs.shape
    ksize = conv_kernel.shape[0]
    pixels = rows * columns
    hidden_units = w_up.shape[1]
    image, upstream = inputs[0], grad_out[0]
    taps = conv_kernel.reshape(ksize * ksize, channels)
    line = lambda v: v.reshape(1, -1)
    vmem = pl.BlockSpec(memory_space=pltpu.VMEM)
    high = rows + ksize - 1
    wide = -(-(columns + 2 * MARGIN) // 8) * 8
    pad = pltpu.VMEM((high, wide, channels), F32)
    shift = pltpu.VMEM((ksize, high, columns, LANES), F32)
    limit = 58 * 1024 * 1024

    gmixed, gwup, gwdown, small = pl.pallas_call(
        functools.partial(block_kernel, rows, columns, ksize),
        out_shape=(
            jax.ShapeDtypeStruct((pixels, channels), F32),
            jax.ShapeDtypeStruct((channels, hidden_units), F32),
            jax.ShapeDtypeStruct((channels, hidden_units), F32),
            jax.ShapeDtypeStruct((16, channels), F32),
        ),
        in_specs=[vmem] * 11,
        out_specs=(vmem,) * 4,
        scratch_shapes=[
            pad,
            shift,
            pltpu.VMEM((pixels, channels), F32),
            pltpu.VMEM((pixels, 1), F32),
            pltpu.VMEM((pixels, channels), BF16),
            pltpu.VMEM((channels, pixels), BF16),
            pltpu.VMEM((pixels, channels), BF16),
            pltpu.VMEM((channels, pixels), BF16),
            pltpu.VMEM((pixels, channels), BF16),
            pltpu.VMEM((pixels, channels), BF16),
            pltpu.VMEM((pixels, channels), F32),
        ],
        compiler_params=pltpu.CompilerParams(vmem_limit_bytes=limit),
    )(
        image,
        upstream.reshape(pixels, channels),
        taps,
        line(conv_bias),
        line(layer_norm_gain),
        line(layer_norm_bias),
        w_up,
        line(up_bias),
        w_down,
        line(down_bias),
        line(layer_scale),
    )

    chunks = 4
    blocks = channels // LANES
    bits = (gx_count - 1).bit_length()
    small_rows = max(blocks * 64, 8 * gx_count * gy_count)
    width = 2 * hidden_units // chunks
    others = gy_count - 1
    slots = 2 * (bits + others)
    back, whole_up, whole_down, whole_small = pl.pallas_call(
        functools.partial(reduce_kernel, gx_count, gy_count, chunks, rows, columns, ksize),
        out_shape=(
            jax.ShapeDtypeStruct((rows, columns, channels), BF16),
            jax.ShapeDtypeStruct((channels, hidden_units), F32),
            jax.ShapeDtypeStruct((channels, hidden_units), F32),
            jax.ShapeDtypeStruct((small_rows, LANES), F32),
        ),
        in_specs=[vmem] * 7,
        out_specs=(vmem,) * 4,
        scratch_shapes=[
            pad,
            pad,
            shift,
            shift,
            pltpu.VMEM((small_rows, LANES), F32),
            pltpu.VMEM((chunks, channels, width), F32),
            pltpu.VMEM((chunks, others) + piece_shape(channels // gx_count, width, gy_count)[1:], F32),
            pltpu.VMEM((small_rows, LANES), F32),
            pltpu.VMEM((others,) + piece_shape(small_rows // gx_count, LANES, gy_count)[1:], F32),
            pltpu.SemaphoreType.DMA((chunks + 1, slots)),
            pltpu.SemaphoreType.DMA((chunks + 1, slots)),
        ],
        compiler_params=pltpu.CompilerParams(
            collective_id=0, has_side_effects=True, vmem_limit_bytes=limit
        ),
    )(gwup, gwdown, small, gmixed.reshape(rows, columns, channels), image, upstream, taps)

    table = jnp.transpose(whole_small[: blocks * 64].reshape(blocks, 64, LANES), (1, 0, 2))
    table = table.reshape(64, channels)
    count = ksize * ksize
    return (
        back[None],
        table[:count].reshape(ksize, ksize, channels),
        table[49],
        table[50],
        table[51],
        whole_up,
        table[54 : 54 + hidden_units // channels].reshape(-1),
        whole_down,
        table[52],
        table[53],
    )


def solution(mesh):
    image = P(("gx", "gy"), None, None, None)
    return jax.shard_map(
        functools.partial(shards, mesh.shape["gx"], mesh.shape["gy"]),
        mesh=mesh,
        in_specs=(image, image) + (P(),) * 9,
        out_specs=(image,) + (P(),) * 9,
        check_vma=False,
    )
```

time: 389 us -> 155 us (0.40)
  waiting for transfers between devices: 176 us -> 0 us
  Pallas kernels: 0 us -> 141 us
  blocking collectives: 73.4 us -> 0 us
  other arithmetic: 67.5 us -> 0 us
  matrix products: 38.5 us -> 0 us
  between operations: 15.9 us -> 0.66 us
    pallas_call x0 -> x2, Pallas kernels: none -> 141 us  [the longest x1 107 us: shards(): pl.pallas_call(functools.partial(reduce_kernel, gx_count, gy_count, chunk...]
    reduce_scatter x4 -> x0, waiting for transfers between devices: 133 us -> none  [the longest x1 55.6 us: shards(): lax.psum_scatter(gw_down, 'gx', scatter_dimension=0, tiled=True)]
    psum x1 -> x0, waiting for transfers between devices: 42.8 us -> none  [shards(): lax.psum((g_kernel, g_cbias, gain_gradient, g_lnbias, g_up_bias, g_down_b...]
    psum x1 -> x0, blocking collectives: 42 us -> none  [shards(): lax.psum((g_kernel, g_cbias, gain_gradient, g_lnbias, g_up_bias, g_down_b...]
    dot_general x6 -> x0, matrix products: 38.5 us -> none  [the longest x1 16.1 us: shards(): jnp.dot(normalized_output, w_up, preferred_element_type=jnp.float32)]
    reshape x1 -> x0, other arithmetic: 37.9 us -> none  [shards(): back.astype(jnp.bfloat16).reshape(1, row_count, column_count, channel_count)]
    all_gather x2 -> x0, blocking collectives: 31.3 us -> none  [the longest x1 17.2 us: shards(): lax.all_gather(parts[0], 'gy', axis=1, tiled=True)]
    reduce_sum x7 -> x0, other arithmetic: 27.7 us -> none  [the longest x1 11.8 us: shards(): mean_removed = mixed - jnp.mean(mixed, axis=-1, keepdims=True)]
  transfers between devices with their start and end apart: 7 -> 0, of which waited for: 5 -> 0; matrix products, arithmetic and copies ran while one was open for 18% -> 0% of each run, Pallas kernels for 0% -> 0%
where the time goes in v1:
time: 155 us
  Pallas kernels  141 us (91%)
  local copies, waits for them, and re-layouts  13.4 us (9%)
    pallas_call x1, Pallas kernels, shards(): pl.pallas_call(functools.partial(reduce_kernel, gx_count, gy_count, chunk...  107 us
    pallas_call x1, Pallas kernels, shards(): pl.pallas_call(functools.partial(block_kernel, rows, columns, ksize), out...  33.9 us
    unnamed x5, local copies, waits for them, and re-layouts  8.93 us

profile of v1, /device:TPU:1, one launch (start us, length us, event | category | flops | bytes accessed | tf_op | source)
XLA Modules:
  0.0 154.6 jit_solution(8091461227799708618)
XLA Ops:
  0.6 1.6 %reshape.68.k_ref = f32[49,512]{1,0:T(8,128)} reshape(f32[7,7,512]{2,1,0:T(8,128)} %param.13) | data formatting | bytes 200704 | tf_op jit(solution)/shard_map/reshape | solution.py:412
  2.2 33.9 %shard_map.186 = (f32[768,512]{1,0:T(8,128)}, f32[512,2048]{1,0:T(8,128)}, f32[512,2048]{1,0:T(8,128)}, f32[16,512]{1,0:T(8,128)}) custom-call(bf16[16,48,512]{2,1,0:T(8,128)(2,1)} %bitcast.26, bf16[768,512]{1,0:T(8,128)(2,1)} %bitcast.28, f32[49,512]{1,0:T(8,128)} %reshape.68.k_ref, f32[1,512]{1,0:T(1,128)} %bitcast.38, f32[1,512]{1,0:T(1,128)} %bitcast.39, ...), custom_call_target="tpu_custom_call" | custom-call | tf_op jit(solution)/shard_map/pallas_call | solution.py:421
  36.1 106.6 %shard_map.187 = (bf16[16,48,512]{2,1,0:T(8,128)(2,1)}, f32[512,2048]{1,0:T(8,128)}, f32[512,2048]{1,0:T(8,128)}, f32[256,128]{1,0:T(8,128)}) custom-call(f32[512,2048]{1,0:T(8,128)} %get-tuple-element.18.gwup_ref, f32[512,2048]{1,0:T(8,128)} %get-tuple-element.19.gwdown_ref, f32[16,512]{1,0:T(8,128)} %get-tuple-element.20.small_ref, ...), custom_call_target="tpu_custom_call" | custom-call | tf_op jit(solution)/shard_map/pallas_call | solution.py:466
  142.7 1.0 copy.24
  143.7 0.6 slice.39
  144.3 0.6 slice_bitcast_fusion
  144.9 0.7 reshape.77
  145.6 2.1 %copy.28 = bf16[1,16,48,512]{3,2,1,0:T(8,128)(2,1)} copy(bf16[1,16,48,512]{3,2,1,0:T(8,128)(2,1)} %bitcast.31) | data formatting | bytes 1572864
  147.7 0.0 copy-start
  147.7 4.8 %copy.29 = f32[512,2048]{1,0:T(8,128)} copy(f32[512,2048]{1,0:T(8,128)} %get-tuple-element.46) | data formatting | bytes 8388608
  152.6 0.0 copy-done
  152.6 2.0 %copy.30 = f32[512,2048]{1,0:T(8,128)} copy(f32[512,2048]{1,0:T(8,128)S(1)} %copy-done) | data formatting | bytes 8388608
  (1 shorter events, 0.0 us)
Async XLA Ops:
  147.7 4.9 %copy-start = (f32[512,2048]{1,0:T(8,128)S(1)}, f32[512,2048]{1,0:T(8,128)}, u32[]{:S(2)}) copy-start(f32[512,2048]{1,0:T(8,128)} %get-tuple-element.48) | copy-start | bytes 12582916

commit v2 on v1

v2 whole, which is shorter than its diff:
```python
import functools

import jax
import jax.numpy as jnp
from jax import lax
from jax.experimental import pallas as pl
from jax.experimental.pallas import tpu as pltpu
from jax.sharding import PartitionSpec as P

MESH = pl.DeviceIdType.MESH
LANES = 128
MARGIN = 8
F32 = jnp.float32
BF16 = jnp.bfloat16


def fill_padded(pad, rows, columns, half, read):
    pad[...] = jnp.zeros_like(pad)

    def put(h, _):
        pad[h + half, MARGIN : MARGIN + columns, :] = read(h)
        return 0

    lax.fori_loop(0, rows, put, 0)


def fill_shifts(shifts, pad, lanes, ksize, columns):
    half = ksize // 2

    def put(r, _):
        for j in range(ksize):
            start = MARGIN - half + j
            shifts[j, r] = pad[r, start : start + columns, lanes]
        return 0

    lax.fori_loop(0, pad.shape[0], put, 0)


def add_rows(target, at, source, source_at, count, cols):
    def one(r, _):
        to = pl.ds(pl.multiple_of(at + r * 8, 8), 8)
        here = pl.ds(pl.multiple_of(source_at + r * 8, 8), 8)
        target[to, :] += source[here, cols]
        return 0

    lax.fori_loop(0, count // 8, one, 0)


def piece_shape(size, width, parts):
    across = min(parts, width // LANES)
    return across, size * across // parts, width // across


def reduce_steps(gx_count, gy_count, order, acc, out, base, width, recv, zrecv, sends, recvs, pending):
    gi, zi = lax.axis_index("gx"), lax.axis_index("gy")
    fraction = 1.0 / (gx_count * gy_count)
    all_cols = slice(base, base + width)
    slot = [0]

    def send(src, dst, gx_to, gy_to):
        n = slot[0]
        slot[0] += 1
        copy = pltpu.make_async_remote_copy(
            src_ref=src,
            dst_ref=dst,
            send_sem=sends.at[n],
            recv_sem=recvs.at[n],
            device_id=(gx_to, gy_to),
            device_id_type=MESH,
        )
        copy.start()
        pending.append(copy)
        return copy

    def rows_at(at, n):
        return pl.ds(pl.multiple_of(at, 8), n)

    size, at, filled = acc.shape[0], 0, 0
    source, source_at, cols = acc, 0, all_cols
    for b in order:
        bit = (gi // 2**b) % 2
        other = gi + (1 - 2 * bit) * 2**b
        size //= 2
        give = source.at[rows_at(source_at + (1 - bit) * size, size), cols]
        copy = send(give, recv.at[filled : filled + size, :], other, zi)
        yield
        copy.wait_recv()
        add_rows(recv, filled, source, source_at + bit * size, size, cols)
        source, source_at, cols = recv, filled, slice(0, width)
        filled += size
        at = at + bit * size

    across, prows, pcols = piece_shape(size, width, gy_count)

    def piece(ref, z, top, left):
        there = rows_at(top + (z // across) * prows, prows)
        return ref.at[there, pl.ds(pl.multiple_of(left + (z % across) * pcols, LANES), pcols)]

    copies = []
    for d in range(1, gy_count):
        z = (zi + d) % gy_count
        copies.append(send(piece(recv, z, source_at, 0), zrecv.at[d - 1], gi, z))
    yield
    total = piece(recv, zi, source_at, 0)[...]
    for d in range(1, gy_count):
        copies[d - 1].wait_recv()
        total = total + zrecv[d - 1]
    done = piece(out, zi, at, base)
    done[...] = total * fraction
    copies = []
    for d in range(1, gy_count):
        z = (zi + d) % gy_count
        copies.append(send(done, done, gi, z))
    yield
    for copy in copies:
        copy.wait_recv()
    for b in reversed(order):
        bit = (gi // 2**b) % 2
        other = gi + (1 - 2 * bit) * 2**b
        mine = out.at[rows_at(at, size), all_cols]
        copy = send(mine, mine, other, zi)
        at = at - bit * size
        size *= 2
        yield
        copy.wait_recv()


def block_kernel(
    gx_count,
    gy_count,
    rows,
    columns,
    ksize,
    x_ref,
    up_ref,
    k_ref,
    cbias_ref,
    gain_ref,
    lnb_ref,
    wup_ref,
    upb_ref,
    wdown_ref,
    downb_ref,
    scale_ref,
    back_ref,
    up_out,
    down_out,
    small_out,
    pad_x,
    pad_g,
    shifts,
    xhat,
    inv,
    normed,
    normed_t,
    gb,
    gb_t,
    hid,
    gpre,
    gnormed,
    acc_up,
    acc_down,
    acc_small,
    full_up,
    full_down,
    recv,
    zrecv,
    recv_small,
    zrecv_small,
    sends,
    recvs,
    stores,
):
    pixels, channels = xhat.shape
    hidden_units = wup_ref.shape[1]
    half = ksize // 2
    block = channels
    blocks = channels // LANES
    bits = (gx_count - 1).bit_length()
    gi, zi = lax.axis_index("gx"), lax.axis_index("gy")
    barrier = pltpu.get_barrier_semaphore()
    for b in range(bits):
        bit = (gi // 2**b) % 2
        other = gi + (1 - 2 * bit) * 2**b
        pl.semaphore_signal(barrier, inc=1, device_id=(other, zi), device_id_type=MESH)
    for d in range(1, gy_count):
        z = (zi + d) % gy_count
        pl.semaphore_signal(barrier, inc=1, device_id=(gi, z), device_id_type=MESH)

    pending, live = [], []
    orders = ([0] + list(range(1, bits)), [0] + list(range(bits - 1, 0, -1)))

    def begin(n):
        acc, full, out = (
            (acc_down, full_down, down_out) if n % 2 == 0 else (acc_up, full_up, up_out)
        )
        cols = slice((n // 2) * block, (n // 2 + 1) * block)

        def run():
            yield from reduce_steps(
                gx_count, gy_count, orders[n % 2], acc, full, cols.start, block,
                recv.at[n], zrecv.at[n], sends.at[n], recvs.at[n], pending,
            )
            copy = pltpu.make_async_copy(full.at[:, cols], out.at[:, cols], stores.at[n])
            copy.start()
            finals.append(copy)

        return run()

    finals = []

    def advance(*fresh):
        for step in list(fresh) + live:
            try:
                next(step)
            except StopIteration:
                live.remove(step)
        live.extend(fresh)

    def put_small(row, value):
        for cb in range(blocks):
            at = cb * 64 + row
            acc_small[at : at + 1, :] = value[:, cb * LANES : (cb + 1) * LANES]

    fill_padded(pad_x, rows, columns, half, lambda h: x_ref[h].astype(F32))
    pad_g[...] = jnp.zeros_like(pad_g)
    acc_small[...] = jnp.zeros_like(acc_small)
    for cb in range(blocks):
        lanes = slice(cb * LANES, (cb + 1) * LANES)
        fill_shifts(shifts, pad_x, lanes, ksize, columns)

        def conv_row(h, _):
            total = jnp.zeros((columns, LANES), F32) + cbias_ref[:, lanes]
            for i in range(ksize):
                for j in range(ksize):
                    tap = i * ksize + j
                    total = total + shifts[j, h + i] * k_ref[tap : tap + 1, lanes]
            xhat[pl.ds(pl.multiple_of(h * columns, 8), columns), lanes] = total
            return 0

        lax.fori_loop(0, rows, conv_row, 0)

    step = columns * 2
    gain = gain_ref[...]

    def norm_rows(b, carry):
        sum_up, sum_gb = carry
        at = pl.ds(pl.multiple_of(b * step, 16), step)
        mixed = xhat[at, :]
        removed = mixed - jnp.mean(mixed, axis=-1, keepdims=True)
        deviation = lax.rsqrt(jnp.mean(removed * removed, axis=-1, keepdims=True) + 1e-06)
        standard = removed * deviation
        xhat[at, :] = standard
        inv[at, :] = deviation
        normed[at, :] = (standard * gain + lnb_ref[...]).astype(BF16)
        upstream = up_ref[at, :].astype(F32)
        g_branch = (upstream * scale_ref[...]).astype(BF16)
        gb[at, :] = g_branch
        sum_up = sum_up + jnp.sum(upstream, axis=0, keepdims=True)
        sum_gb = sum_gb + jnp.sum(g_branch.astype(F32), axis=0, keepdims=True)
        return sum_up, sum_gb

    zero = jnp.zeros((1, channels), F32)
    sum_up, sum_gb = lax.fori_loop(0, pixels // step, norm_rows, (zero, zero))
    normed_t[...] = jnp.transpose(normed[...].astype(F32)).astype(BF16)
    gb_t[...] = jnp.transpose(gb[...].astype(F32)).astype(BF16)
    gnormed[...] = jnp.zeros_like(gnormed)
    put_small(52, sum_gb)
    tall = pixels // 3

    folded = jnp.zeros((channels, LANES), F32)
    for fb in range(hidden_units // block):
        cols = slice(fb * block, (fb + 1) * block)
        bias = upb_ref[:, cols]

        def mlp_rows(b, total):
            at = pl.ds(pl.multiple_of(b * tall, 16), tall)
            pre = jnp.dot(normed[at, :], wup_ref[:, cols], preferred_element_type=F32) + bias
            cdf = 0.5 * (1.0 + lax.erf(pre * 0.7071067811865476))
            hid[at, :] = (pre * cdf).astype(BF16)
            slope = cdf + pre * (jnp.exp(-0.5 * pre * pre) * 0.3989422804014327)
            g_hidden = jnp.dot(gb[at, :], wdown_ref[:, cols], preferred_element_type=F32)
            g = (g_hidden * slope).astype(BF16)
            gpre[at, :] = g
            gnormed[at, :] += lax.dot_general(
                g, wup_ref[:, cols], (((1,), (1,)), ((), ())), preferred_element_type=F32
            )
            return total + jnp.sum(g.astype(F32), axis=0, keepdims=True)

        total = lax.fori_loop(0, 3, mlp_rows, jnp.zeros((1, block), F32))
        put_small(54 + fb, total)
        acc_up[:, cols] = jnp.dot(normed_t[...], gpre[...], preferred_element_type=F32)
        gw = jnp.dot(gb_t[...], hid[...], preferred_element_type=F32)
        acc_down[:, cols] = gw
        if fb == 0:
            pl.semaphore_wait(barrier, bits + gy_count - 1)
        advance(begin(2 * fb), begin(2 * fb + 1))
        product = gw * wdown_ref[:, cols].astype(F32)
        for part in range(block // LANES):
            folded = folded + product[:, part * LANES : (part + 1) * LANES]

    scale_sum = jnp.sum(jnp.transpose(folded), axis=0, keepdims=True)
    put_small(53, scale_sum / scale_ref[...] + downb_ref[...] * sum_up)

    def back_rows(h, carry):
        s_gain, s_bias, s_conv = carry
        at = pl.ds(pl.multiple_of(h * columns, 16), columns)
        g, standard = gnormed[at, :], xhat[at, :]
        gx = g * gain
        mean_g = jnp.mean(gx, axis=-1, keepdims=True)
        mean_gx = jnp.mean(gx * standard, axis=-1, keepdims=True)
        gm = inv[at, :] * (gx - mean_g - standard * mean_gx)
        pad_g[h + half, MARGIN : MARGIN + columns, :] = gm
        return (
            s_gain + jnp.sum(g * standard, axis=0, keepdims=True),
            s_bias + jnp.sum(g, axis=0, keepdims=True),
            s_conv + jnp.sum(gm, axis=0, keepdims=True),
        )

    s_gain, s_bias, s_conv = lax.fori_loop(0, rows, back_rows, (zero, zero, zero))
    put_small(49, s_conv)
    put_small(50, s_gain)
    put_small(51, s_bias)
    advance()

    for cb in range(blocks):
        lanes = slice(cb * LANES, (cb + 1) * LANES)
        base = cb * 64
        fill_shifts(shifts, pad_x, lanes, ksize, columns)
        for j in range(ksize):

            def kernel_row(h, sums):
                g = pad_g[h + half, MARGIN : MARGIN + columns, lanes]
                new = []
                for i in range(ksize):
                    p = g * shifts[j, h + i]
                    part = p[0:8]
                    for w in range(8, columns, 8):
                        part = part + p[w : w + 8]
                    new.append(sums[i] + part)
                return tuple(new)

            zeros = tuple(jnp.zeros((8, LANES), F32) for _ in range(ksize))
            sums = lax.fori_loop(0, rows, kernel_row, zeros)
            for i in range(ksize):
                row = base + i * ksize + j
                acc_small[row : row + 1, :] = jnp.sum(sums[i], axis=0, keepdims=True)
        if cb == blocks - 1:
            advance(
                reduce_steps(
                    gx_count, gy_count, orders[0], acc_small, small_out, 0, LANES,
                    recv_small, zrecv_small, sends.at[sends.shape[0] - 1],
                    recvs.at[recvs.shape[0] - 1], pending,
                )
            )
        elif cb % 2 == 1:
            advance()

    for cb in range(blocks):
        lanes = slice(cb * LANES, (cb + 1) * LANES)
        fill_shifts(shifts, pad_g, lanes, ksize, columns)

        def back_row(h, _):
            at = pl.ds(pl.multiple_of(h * columns, 16), columns)
            total = up_ref[at, lanes].astype(F32)
            for i in range(ksize):
                for j in range(ksize):
                    tap = i * ksize + j
                    total = total + (
                        shifts[ksize - 1 - j, h + (ksize - 1 - i)] * k_ref[tap : tap + 1, lanes]
                    )
            back_ref[at, lanes] = total.astype(BF16)
            return 0

        lax.fori_loop(0, rows, back_row, 0)
        advance()

    while live:
        advance()
    for copy in pending:
        copy.wait_send()
    for copy in finals:
        copy.wait()


def finish_kernel(
    ksize,
    up_ref,
    down_ref,
    back_ref,
    small_ref,
    back_out,
    kernel_out,
    cbias_out,
    gain_out,
    lnb_out,
    up_out,
    upb_out,
    down_out,
    downb_out,
    scale_out,
    sems,
):
    parts = 4
    tall = up_ref.shape[0] // parts
    copies = [pltpu.make_async_copy(back_ref, back_out, sems.at[2 * parts])]
    for n in range(parts):
        at = slice(n * tall, (n + 1) * tall)
        copies.append(pltpu.make_async_copy(up_ref.at[at], up_out.at[at], sems.at[2 * n]))
        copies.append(pltpu.make_async_copy(down_ref.at[at], down_out.at[at], sems.at[2 * n + 1]))
    for copy in copies:
        copy.start()
    channels = up_ref.shape[0]
    for cb in range(channels // LANES):
        base, lanes = cb * 64, slice(cb * LANES, (cb + 1) * LANES)
        for i in range(ksize):
            row = base + i * ksize
            kernel_out[i, :, lanes] = small_ref[row : row + ksize, :]
        for n, out in enumerate((cbias_out, gain_out, lnb_out, downb_out, scale_out)):
            out[:, lanes] = small_ref[base + 49 + n : base + 50 + n, :]
        for fb in range(up_ref.shape[1] // channels):
            to = fb * channels + cb * LANES
            upb_out[:, to : to + LANES] = small_ref[base + 54 + fb : base + 55 + fb, :]
    for copy in copies:
        copy.wait()


def shards(
    gx_count,
    gy_count,
    inputs,
    grad_out,
    conv_kernel,
    conv_bias,
    layer_norm_gain,
    layer_norm_bias,
    w_up,
    up_bias,
    w_down,
    down_bias,
    layer_scale,
):
    _, rows, columns, channels = inputs.shape
    ksize = conv_kernel.shape[0]
    pixels = rows * columns
    hidden_units = w_up.shape[1]
    taps = conv_kernel.reshape(ksize * ksize, channels)
    line = lambda v: v.reshape(1, -1)
    vmem = pl.BlockSpec(memory_space=pltpu.VMEM)
    anywhere = pl.BlockSpec(memory_space=pl.ANY)
    high = rows + ksize - 1
    wide = -(-(columns + 2 * MARGIN) // 8) * 8
    limit = 60 * 1024 * 1024
    blocks = channels // LANES
    bits = (gx_count - 1).bit_length()
    small_rows = max(blocks * 64, 8 * gx_count * gy_count)
    chunks = 2 * hidden_units // channels
    others = gy_count - 1
    slots = 2 * (bits + others)
    left = channels // gx_count
    weight = jax.ShapeDtypeStruct((channels, hidden_units), F32)
    wide_rows = pltpu.VMEM((pixels, channels), F32)
    narrow_rows = pltpu.VMEM((pixels, channels), BF16)
    turned_rows = pltpu.VMEM((channels, pixels), BF16)
    whole = pltpu.VMEM((channels, hidden_units), F32)
    back, whole_up, whole_down, whole_small = pl.pallas_call(
        functools.partial(block_kernel, gx_count, gy_count, rows, columns, ksize),
        out_shape=(
            jax.ShapeDtypeStruct((pixels, channels), BF16),
            weight,
            weight,
            jax.ShapeDtypeStruct((small_rows, LANES), F32),
        ),
        in_specs=[vmem] * 11,
        out_specs=(vmem, anywhere, anywhere, vmem),
        scratch_shapes=[
            pltpu.VMEM((high, wide, channels), F32),
            pltpu.VMEM((high, wide, channels), F32),
            pltpu.VMEM((ksize, high, columns, LANES), F32),
            wide_rows,
            pltpu.VMEM((pixels, 1), F32),
            narrow_rows,
            turned_rows,
            narrow_rows,
            turned_rows,
            narrow_rows,
            narrow_rows,
            wide_rows,
            whole,
            whole,
            pltpu.VMEM((small_rows, LANES), F32),
            whole,
            whole,
            pltpu.VMEM((chunks, channels - left, channels), F32),
            pltpu.VMEM((chunks, others) + piece_shape(left, channels, gy_count)[1:], F32),
            pltpu.VMEM((small_rows, LANES), F32),
            pltpu.VMEM((others,) + piece_shape(small_rows // gx_count, LANES, gy_count)[1:], F32),
            pltpu.SemaphoreType.DMA((chunks + 1, slots)),
            pltpu.SemaphoreType.DMA((chunks + 1, slots)),
            pltpu.SemaphoreType.DMA((chunks,)),
        ],
        compiler_params=pltpu.CompilerParams(
            collective_id=0, has_side_effects=True, vmem_limit_bytes=limit
        ),
    )(
        inputs[0],
        grad_out.reshape(pixels, channels),
        taps,
        line(conv_bias),
        line(layer_norm_gain),
        line(layer_norm_bias),
        w_up,
        line(up_bias),
        w_down,
        line(down_bias),
        line(layer_scale),
    )

    one = jax.ShapeDtypeStruct((1, channels), F32)
    results = pl.pallas_call(
        functools.partial(finish_kernel, ksize),
        out_shape=(
            jax.ShapeDtypeStruct((pixels, channels), BF16),
            jax.ShapeDtypeStruct(conv_kernel.shape, F32),
            one,
            one,
            one,
            weight,
            jax.ShapeDtypeStruct((1, hidden_units), F32),
            weight,
            one,
            one,
        ),
        in_specs=[anywhere, anywhere, anywhere, vmem],
        out_specs=(anywhere, vmem, vmem, vmem, vmem, anywhere, vmem, anywhere, vmem, vmem),
        scratch_shapes=[pltpu.SemaphoreType.DMA((9,))],
        compiler_params=pltpu.CompilerParams(vmem_limit_bytes=limit),
    )(whole_up, whole_down, back, whole_small)
    grad_inputs, g_kernel, cbias, ln_gain, lnb, g_up, upb, g_down, downb, scale = results
    flat = lambda v: v.reshape(-1)
    return (
        grad_inputs.reshape(inputs.shape),
        g_kernel,
        flat(cbias),
        flat(ln_gain),
        flat(lnb),
        g_up,
        flat(upb),
        g_down,
        flat(downb),
        flat(scale),
    )


def solution(mesh):
    image = P(("gx", "gy"), None, None, None)
    return jax.shard_map(
        functools.partial(shards, mesh.shape["gx"], mesh.shape["gy"]),
        mesh=mesh,
        in_specs=(image, image) + (P(),) * 9,
        out_specs=(image,) + (P(),) * 9,
        check_vma=False,
    )
```

time: 155 us -> 399 us (2.57)
  Pallas kernels: 141 us -> 397 us
  local copies, waits for them, and re-layouts: 13.4 us -> 1.56 us
    pallas_call x2, Pallas kernels: 141 us -> 397 us  [the longest x1 281 us: shards(): pl.pallas_call(functools.partial(finish_kernel, ksize), out_shape=(jax.Sh...]
    unnamed x5 -> x0, local copies, waits for them, and re-layouts: 8.93 us -> none
where the time goes in v2:
time: 399 us
  Pallas kernels  397 us (99%)
    pallas_call x1, Pallas kernels, shards(): pl.pallas_call(functools.partial(finish_kernel, ksize), out_shape=(jax.Sh...  281 us
    pallas_call x1, Pallas kernels, shards(): pl.pallas_call(functools.partial(block_kernel, gx_count, gy_count, rows,...  116 us

profile of v2, /device:TPU:1, one launch (start us, length us, event | category | flops | bytes accessed | tf_op | source)
XLA Modules:
  0.0 398.9 jit_solution(7030645762312377589)
XLA Ops:
  0.6 1.6 reshape.66.k_ref
  2.2 116.0 %shard_map.186 = (bf16[768,512]{1,0:T(8,128)(2,1)}, f32[512,2048]{1,0:T(8,128)}, f32[512,2048]{1,0:T(8,128)}, f32[256,128]{1,0:T(8,128)}) custom-call(bf16[16,48,512]{2,1,0:T(8,128)(2,1)} %bitcast.15, bf16[768,512]{1,0:T(8,128)(2,1)} %bitcast.16, f32[49,512]{1,0:T(8,128)} %reshape.66.k_ref, f32[1,512]{1,0:T(1,128)} %bitcast.18, f32[1,512]{1,0:T(1,128)} %bitcast.19, ...), custom_call_target="tpu_custom_call" | custom-call | tf_op jit(solution)/shard_map/pallas_call | solution.py:466
  118.2 280.7 %shard_map.187 = (bf16[768,512]{1,0:T(8,128)(2,1)}, f32[7,7,512]{2,1,0:T(8,128)}, f32[1,512]{1,0:T(1,128)}, f32[1,512]{1,0:T(1,128)}, f32[1,512]{1,0:T(1,128)}, ...) custom-call(f32[512,2048]{1,0:T(8,128)} %get-tuple-element.24.up_ref,, ...), custom_call_target="tpu_custom_call" | custom-call | tf_op jit(solution)/shard_map/pallas_call | solution.py:520

commit v3 on v2

--- a/solution.py
+++ b/solution.py
@@ -215,7 +215,7 @@
                 next(step)
             except StopIteration:
                 live.remove(step)
-        live.extend(fresh)
+        live[:0] = fresh
 
     def put_small(row, value):
         for cb in range(blocks):
@@ -233,8 +233,7 @@
             total = jnp.zeros((columns, LANES), F32) + cbias_ref[:, lanes]
             for i in range(ksize):
                 for j in range(ksize):
-                    tap = i * ksize + j
-                    total = total + shifts[j, h + i] * k_ref[tap : tap + 1, lanes]
+                    total = total + shifts[j, h + i] * k_ref[i, j : j + 1, lanes]
             xhat[pl.ds(pl.multiple_of(h * columns, 8), columns), lanes] = total
             return 0
 
@@ -321,7 +320,6 @@
     put_small(49, s_conv)
     put_small(50, s_gain)
     put_small(51, s_bias)
-    advance()
 
     for cb in range(blocks):
         lanes = slice(cb * LANES, (cb + 1) * LANES)
@@ -365,9 +363,8 @@
             total = up_ref[at, lanes].astype(F32)
             for i in range(ksize):
                 for j in range(ksize):
-                    tap = i * ksize + j
                     total = total + (
-                        shifts[ksize - 1 - j, h + (ksize - 1 - i)] * k_ref[tap : tap + 1, lanes]
+                        shifts[ksize - 1 - j, h + (ksize - 1 - i)] * k_ref[i, j : j + 1, lanes]
                     )
             back_ref[at, lanes] = total.astype(BF16)
             return 0
@@ -399,16 +396,24 @@
     down_out,
     downb_out,
     scale_out,
+    up_hold,
+    down_hold,
+    back_hold,
     sems,
 ):
-    parts = 4
+    parts = up_hold.shape[0]
     tall = up_ref.shape[0] // parts
-    copies = [pltpu.make_async_copy(back_ref, back_out, sems.at[2 * parts])]
+    pairs = []
     for n in range(parts):
         at = slice(n * tall, (n + 1) * tall)
-        copies.append(pltpu.make_async_copy(up_ref.at[at], up_out.at[at], sems.at[2 * n]))
-        copies.append(pltpu.make_async_copy(down_ref.at[at], down_out.at[at], sems.at[2 * n + 1]))
-    for copy in copies:
+        pairs.append((up_ref.at[at], up_hold.at[n], up_out.at[at]))
+        pairs.append((down_ref.at[at], down_hold.at[n], down_out.at[at]))
+    pairs.append((back_ref, back_hold, back_out))
+    reads, copies = [], []
+    for n, (source, hold, target) in enumerate(pairs):
+        reads.append(pltpu.make_async_copy(source, hold, sems.at[0, n]))
+        copies.append(pltpu.make_async_copy(hold, target, sems.at[1, n]))
+    for copy in reads:
         copy.start()
     channels = up_ref.shape[0]
     for cb in range(channels // LANES):
@@ -421,6 +426,9 @@
         for fb in range(up_ref.shape[1] // channels):
             to = fb * channels + cb * LANES
             upb_out[:, to : to + LANES] = small_ref[base + 54 + fb : base + 55 + fb, :]
+    for read, copy in zip(reads, copies):
+        read.wait()
+        copy.start()
     for copy in copies:
         copy.wait()
 
@@ -444,7 +452,6 @@
     ksize = conv_kernel.shape[0]
     pixels = rows * columns
     hidden_units = w_up.shape[1]
-    taps = conv_kernel.reshape(ksize * ksize, channels)
     line = lambda v: v.reshape(1, -1)
     vmem = pl.BlockSpec(memory_space=pltpu.VMEM)
     anywhere = pl.BlockSpec(memory_space=pl.ANY)
@@ -505,7 +512,7 @@
     )(
         inputs[0],
         grad_out.reshape(pixels, channels),
-        taps,
+        conv_kernel,
         line(conv_bias),
         line(layer_norm_gain),
         line(layer_norm_bias),
@@ -516,6 +523,7 @@
         line(layer_scale),
     )
 
+    parts = 4
     one = jax.ShapeDtypeStruct((1, channels), F32)
     results = pl.pallas_call(
         functools.partial(finish_kernel, ksize),
@@ -533,7 +541,12 @@
         ),
         in_specs=[anywhere, anywhere, anywhere, vmem],
         out_specs=(anywhere, vmem, vmem, vmem, vmem, anywhere, vmem, anywhere, vmem, vmem),
-        scratch_shapes=[pltpu.SemaphoreType.DMA((9,))],
+        scratch_shapes=[
+            pltpu.VMEM((parts, channels // parts, hidden_units), F32),
+            pltpu.VMEM((parts, channels // parts, hidden_units), F32),
+            narrow_rows,
+            pltpu.SemaphoreType.DMA((2, 2 * parts + 1)),
+        ],
         compiler_params=pltpu.CompilerParams(vmem_limit_bytes=limit),
     )(whole_up, whole_down, back, whole_small)
     grad_inputs, g_kernel, cbias, ln_gain, lnb, g_up, upb, g_down, downb, scale = results

time: 399 us -> 126 us (0.32)
  Pallas kernels: 397 us -> 125 us
    pallas_call x1, Pallas kernels: 281 us -> 8.46 us  [shards(): pl.pallas_call(functools.partial(finish_kernel, ksize), out_shape=(jax.Sh...]
where the time goes in v3:
time: 126 us
  Pallas kernels  125 us (99%)
    pallas_call x1, Pallas kernels, shards(): pl.pallas_call(functools.partial(block_kernel, gx_count, gy_count, rows,...  117 us
    pallas_call x1, Pallas kernels, shards(): pl.pallas_call(functools.partial(finish_kernel, ksize), out_shape=(jax.Sh...  8.46 us

profile of v3, /device:TPU:1, one launch (start us, length us, event | category | flops | bytes accessed | tf_op | source)
XLA Modules:
  0.0 126.0 jit_solution(6265997507542968936)
XLA Ops:
  0.6 116.9 %shard_map.186 = (bf16[768,512]{1,0:T(8,128)(2,1)}, f32[512,2048]{1,0:T(8,128)}, f32[512,2048]{1,0:T(8,128)}, f32[256,128]{1,0:T(8,128)}) custom-call(bf16[16,48,512]{2,1,0:T(8,128)(2,1)} %bitcast.15, bf16[768,512]{1,0:T(8,128)(2,1)} %bitcast.16, f32[7,7,512]{2,1,0:T(8,128)} %k_ref.1, f32[1,512]{1,0:T(1,128)} %bitcast.18, f32[1,512]{1,0:T(1,128)} %bitcast.19, ...), custom_call_target="tpu_custom_call" | custom-call | tf_op jit(solution)/shard_map/pallas_call | solution.py:473
  117.5 8.5 %shard_map.187 = (bf16[768,512]{1,0:T(8,128)(2,1)}, f32[7,7,512]{2,1,0:T(8,128)}, f32[1,512]{1,0:T(1,128)}, f32[1,512]{1,0:T(1,128)}, f32[1,512]{1,0:T(1,128)}, ...) custom-call(f32[512,2048]{1,0:T(8,128)} %get-tuple-element.24.up_ref,, ...), custom_call_target="tpu_custom_call" | custom-call | tf_op jit(solution)/shard_map/pallas_call | solution.py:528

commit v4 on v3

--- a/solution.py
+++ b/solution.py
@@ -33,17 +33,19 @@
             shifts[j, r] = pad[r, start : start + columns, lanes]
         return 0
 
-    lax.fori_loop(0, pad.shape[0], put, 0)
+    lax.fori_loop(0, pad.shape[0], put, 0, unroll=2)
 
 
 def add_rows(target, at, source, source_at, count, cols):
+    tall = 32 if count % 32 == 0 else 8
+
     def one(r, _):
-        to = pl.ds(pl.multiple_of(at + r * 8, 8), 8)
-        here = pl.ds(pl.multiple_of(source_at + r * 8, 8), 8)
+        to = pl.ds(pl.multiple_of(at + r * tall, 8), tall)
+        here = pl.ds(pl.multiple_of(source_at + r * tall, 8), tall)
         target[to, :] += source[here, cols]
         return 0
 
-    lax.fori_loop(0, count // 8, one, 0)
+    lax.fori_loop(0, count // tall, one, 0)
 
 
 def piece_shape(size, width, parts):
@@ -286,7 +288,7 @@
             )
             return total + jnp.sum(g.astype(F32), axis=0, keepdims=True)
 
-        total = lax.fori_loop(0, 3, mlp_rows, jnp.zeros((1, block), F32))
+        total = lax.fori_loop(0, 3, mlp_rows, jnp.zeros((1, block), F32), unroll=3)
         put_small(54 + fb, total)
         acc_up[:, cols] = jnp.dot(normed_t[...], gpre[...], preferred_element_type=F32)
         gw = jnp.dot(gb_t[...], hid[...], preferred_element_type=F32)
@@ -316,10 +318,11 @@
             s_conv + jnp.sum(gm, axis=0, keepdims=True),
         )
 
-    s_gain, s_bias, s_conv = lax.fori_loop(0, rows, back_rows, (zero, zero, zero))
+    s_gain, s_bias, s_conv = lax.fori_loop(0, rows, back_rows, (zero, zero, zero), unroll=2)
     put_small(49, s_conv)
     put_small(50, s_gain)
     put_small(51, s_bias)
+    advance()
 
     for cb in range(blocks):
         lanes = slice(cb * LANES, (cb + 1) * LANES)
@@ -339,7 +342,7 @@
                 return tuple(new)
 
             zeros = tuple(jnp.zeros((8, LANES), F32) for _ in range(ksize))
-            sums = lax.fori_loop(0, rows, kernel_row, zeros)
+            sums = lax.fori_loop(0, rows, kernel_row, zeros, unroll=4)
             for i in range(ksize):
                 row = base + i * ksize + j
                 acc_small[row : row + 1, :] = jnp.sum(sums[i], axis=0, keepdims=True)
@@ -351,7 +354,7 @@
                     recvs.at[recvs.shape[0] - 1], pending,
                 )
             )
-        elif cb % 2 == 1:
+        else:
             advance()
 
     for cb in range(blocks):
@@ -369,7 +372,9 @@
             back_ref[at, lanes] = total.astype(BF16)
             return 0
 
-        lax.fori_loop(0, rows, back_row, 0)
+        lax.fori_loop(0, rows // 2, back_row, 0)
+        advance()
+        lax.fori_loop(rows // 2, rows, back_row, 0)
         advance()
 
     while live:

time: 126 us -> 136 us (1.079)
  Pallas kernels: 125 us -> 135 us
    pallas_call x1, Pallas kernels: 117 us -> 126 us  [shards(): pl.pallas_call(functools.partial(block_kernel, gx_count, gy_count, rows,...]
where the time goes in v4:
time: 136 us; the launch traced here: 135 us
  Pallas kernels  135 us (99%)
    pallas_call x1, Pallas kernels, shards(): pl.pallas_call(functools.partial(block_kernel, gx_count, gy_count, rows,...  126 us
    pallas_call x1, Pallas kernels, shards(): pl.pallas_call(functools.partial(finish_kernel, ksize), out_shape=(jax.Sh...  8.46 us

profile of v4, /device:TPU:1, one launch (start us, length us, event | category | flops | bytes accessed | tf_op | source)
XLA Modules:
  0.0 135.3 jit_solution(1636397465002297127)
XLA Ops:
  0.6 126.0 %shard_map.186 = (bf16[768,512]{1,0:T(8,128)(2,1)}, f32[512,2048]{1,0:T(8,128)}, f32[512,2048]{1,0:T(8,128)}, f32[256,128]{1,0:T(8,128)}) custom-call(bf16[16,48,512]{2,1,0:T(8,128)(2,1)} %bitcast.15, bf16[768,512]{1,0:T(8,128)(2,1)} %bitcast.16, f32[7,7,512]{2,1,0:T(8,128)} %k_ref.1, f32[1,512]{1,0:T(1,128)} %bitcast.18, f32[1,512]{1,0:T(1,128)} %bitcast.19, ...), custom_call_target="tpu_custom_call" | custom-call | tf_op jit(solution)/shard_map/pallas_call | solution.py:478
  126.7 8.5 %shard_map.187 = (bf16[768,512]{1,0:T(8,128)(2,1)}, f32[7,7,512]{2,1,0:T(8,128)}, f32[1,512]{1,0:T(1,128)}, f32[1,512]{1,0:T(1,128)}, f32[1,512]{1,0:T(1,128)}, ...) custom-call(f32[512,2048]{1,0:T(8,128)} %get-tuple-element.24.up_ref,, ...), custom_call_target="tpu_custom_call" | custom-call | tf_op jit(solution)/shard_map/pallas_call | solution.py:533
